TPU v7x, 256 devices: a whole 4x4x8 slice. The times are simulated.
256 devices in a mesh: seq: 32 (over z, x), dp: 8 (over y, core).
Axes of the slice: x: 4, y: 4, z: 8, core: 2. Of those that a mesh axis runs over, the one named last changes fastest.
Arguments:
- queries: bfloat16 [8, 4096, 1024], P('dp', 'seq'), may hold values from -40 to 40
- keys: bfloat16 [8, 4096, 1024], P('dp', 'seq'), may hold values from -4 to 4
- values: bfloat16 [8, 4096, 1024], P('dp', 'seq'), may hold values from -6 to 6
- d_out: bfloat16 [8, 4096, 1024], P('dp', 'seq'), may hold values from -6 to 6
- w_out: bfloat16 [1024, 1024], replicated, may hold values from -0.1875 to 0.1875
Outputs:
- d_queries: bfloat16 [8, 4096, 1024], P('dp', 'seq')
- d_keys: bfloat16 [8, 4096, 1024], P('dp', 'seq')
- d_values: bfloat16 [8, 4096, 1024], P('dp', 'seq')
- grad_w_out: float32 [1024, 1024], P('seq', 'dp')
All inputs are finite; a program needn't handle non-finite values.
Results may differ from a plain program's by a relative error of at most 0.017.
Values may be sent and summed in bfloat16 or wider, within the bound.
A program may use at most 128 MiB of HBM per device.

v0:
```python
import jax
import jax.numpy as jnp
from jax import lax
from jax.experimental import pallas as pl
from jax.experimental.pallas import tpu as pltpu
from jax.sharding import PartitionSpec as P

ROWS = 128
WIDTH = 1024
PAIR = 128
PAIRS = 8
KEYS = 384
N_SEQ = 32
X, Z = 4, 8
FACTOR = 32768 ** (-0.5)
STEPS = 4
SENT = 80
WIDE = 256
VMEM_BYTES = 56 * 1024 * 1024
MESH = pl.DeviceIdType.MESH
F32 = jnp.float32
BF16 = jnp.bfloat16

OWN1, OWN2, LEFT, RIGHT, LEFT4, RIGHT4 = 128, 192, 224, 288, 352, 368


def dot_nt(a, b):
    return lax.dot_general(a, b, (((1,), (1,)), ((), ())), preferred_element_type=F32)


def dot_tn(a, b):
    return lax.dot_general(a, b, (((0,), (0,)), ((), ())), preferred_element_type=F32)


def dot_nn(a, b):
    return lax.dot_general(a, b, (((1,), (0,)), ((), ())), preferred_element_type=F32)


def two_heads(block, scale):
    lane = lax.broadcasted_iota(jnp.int32, (1, PAIR), 1)
    first = jnp.where(lane < 64, scale, 0.0).astype(BF16)
    second = jnp.where(lane < 64, 0.0, scale).astype(BF16)
    return jnp.concatenate([block * first, block * second], axis=0)


def one_of_two(both):
    row = lax.broadcasted_iota(jnp.int32, (PAIR, ROWS), 0)
    return jnp.where(row < 64, both[:, :ROWS], both[:, ROWS:])


def pool_matrix():
    row = lax.broadcasted_iota(jnp.int32, (ROWS, ROWS), 0)
    token = lax.broadcasted_iota(jnp.int32, (ROWS, ROWS), 1)
    level = jnp.where(row < 64, 1, jnp.where(row < 96, 2, jnp.where(row < 112, 3, 4)))
    base = jnp.where(row < 64, 0, jnp.where(row < 96, 64, jnp.where(row < 112, 96, 112)))
    matrix = jnp.where(lax.shift_right_logical(token, level) == row - base, 1.0, 0.0).astype(BF16)
    row = lax.broadcasted_iota(jnp.int32, (ROWS, 1), 0)
    scale = jnp.where(
        row < 64, 2.0 ** (-0.5), jnp.where(row < 96, 0.5, jnp.where(row < 112, 2.0 ** (-1.5), 0.25))
    ).astype(F32)
    return matrix, scale


def rim_row(row, side):
    level = lax.rem(row, 64) // 16
    within = lax.rem(row, 16)
    if side == 0:
        within = within + jnp.where(level == 0, 112, jnp.where(level == 1, 48, jnp.where(level == 2, 16, 0)))
    return row // 64, level, within


def sent_row(row, side):
    fine = row < 32
    level = jnp.where(fine, 0, (row - 16) // 16)
    part = jnp.where(fine, row // 16, lax.rem(row, 16) // 8)
    within = jnp.where(fine, lax.rem(row, 16), lax.rem(row, 8))
    if side == 0:
        base = jnp.where(fine, 112, jnp.where(level == 1, 48, jnp.where(level == 2, 16, 0)))
    else:
        base = jnp.where(fine, 0, 8)
    return part, level, lax.shift_left(base + within, level)


def rim_matrix(shape, rim_axis, side):
    part, level, position = rim_row(lax.broadcasted_iota(jnp.int32, shape, rim_axis), side)
    from_part, _, first = sent_row(lax.broadcasted_iota(jnp.int32, shape, 1 - rim_axis), side)
    covered = (part == from_part) & (lax.shift_right_logical(first, level) == position)
    return jnp.where(covered, 1.0, 0.0).astype(BF16)


def level_scale(level):
    return jnp.where(
        level == 0, 1.0, jnp.where(level == 1, 2.0 ** (-0.5), jnp.where(level == 2, 0.5, 2.0 ** (-1.5)))
    ).astype(F32)


def rim_scale(side):
    _, level, position = rim_row(lax.broadcasted_iota(jnp.int32, (ROWS, 1), 0), side)
    token = lax.shift_left(position, level)
    if side == 0:
        source = jnp.where(token >= 112, 0, jnp.where(token >= 96, 1, jnp.where(token >= 64, 2, 3)))
    else:
        source = jnp.where(token < 16, 0, jnp.where(token < 32, 1, jnp.where(token < 64, 2, 3)))
    return level_scale(level - source)


def spread_matrix():
    token = lax.broadcasted_iota(jnp.int32, (ROWS, ROWS), 0)
    row = lax.broadcasted_iota(jnp.int32, (ROWS, ROWS), 1)
    level = jnp.where(row < 64, 1, jnp.where(row < 96, 2, 4))
    target = jnp.where(row < 64, row, jnp.where(row < 96, row - 64, lax.rem(row - 96, 8)))
    return jnp.where(lax.shift_right_logical(token, level) == target, 1.0, 0.0).astype(BF16)


def spread_sent(part):
    columns = []
    for side in (0, 1):
        token = lax.broadcasted_iota(jnp.int32, (ROWS, SENT), 0)
        of_part, level, first = sent_row(lax.broadcasted_iota(jnp.int32, (ROWS, SENT), 1), side)
        same = lax.shift_right_logical(token, level) == lax.shift_right_logical(first, level)
        columns.append(jnp.where((of_part == part) & same, 1.0, 0.0))
    return columns


def fill_bias(bias, device):
    token = lax.rem(lax.broadcasted_iota(jnp.int32, (16, 2 * ROWS), 1), ROWS)
    not_first = device > 0
    not_last = device < N_SEQ - 1

    def put(row, valid):
        bias[row : row + 16, :] = jnp.where(valid, 0.0, -1e30).astype(F32)

    for block in range(8):
        near = token // 16 - block
        put(16 * block, (near >= -1) & (near <= 1))
    for block in range(4):
        near = token // 32 - block
        put(OWN1 + 16 * block, (near == -1) | (near == 1))
    for block in range(2):
        put(OWN2 + 16 * block, token // 64 != block)
    for level in range(4):
        span = 16 * 2**level
        put(LEFT + 16 * level, (token < span) & not_first)
        put(RIGHT + 16 * level, (token >= ROWS - span) & not_last)
    always = token >= 0
    put(LEFT4, always & (device >= 2))
    put(RIGHT4, always & (device < N_SEQ - 2))


def kernel(
    q_hbm, k_hbm, v_hbm, d_hbm, w_hbm,
    dq_ref, dk_ref, dv_ref, gw_ref, q, d, w, g, kv, bias, spread, spread_back, unfold, fold,
    rim, rim_in, four, four_in,
    weights, weights_half, grad_scores, own, back, back_in, back_rim, back_four, back_four_in,
    pairs_a, pairs_d, kept, kept2, y1_out, y1_in, y2_out, y2_in, z_out, z_in,
    in_sem, rim_s, rim_r, four_s, four_r, d2_s, d2_r, a_s, a_r, y1_s, y1_r, y2_s, y2_r,
    z_s, z_r, back_s, back_r, bfour_s, bfour_r,
):
    seq = lax.axis_index("seq")
    dp = lax.axis_index("dp")
    z, x = lax.div(seq, X), lax.rem(seq, X)
    y, core = lax.div(dp, 2), lax.rem(dp, 2)
    ya = y + 1 - 2 * lax.rem(y, 2)
    yb = 3 - y
    yo = 3 - ya
    pair_of = lax.div(seq, 2)
    parity = lax.rem(seq, 2)

    def at(seq_to, dp_to):
        return {"seq": seq_to, "dp": dp_to}

    right = at(lax.rem(seq + 1, N_SEQ), dp)
    left = at(lax.rem(seq + N_SEQ - 1, N_SEQ), dp)
    twin = at(seq, 2 * y + 1 - core)
    at_ya = at(seq, 2 * ya + core)
    at_yb = at(seq, 2 * yb + core)
    fours = []
    for side in (0, 1):
        block = lax.rem(pair_of + (N_SEQ // 2 - 1 if side == 0 else 1), N_SEQ // 2)
        for part in (0, 1):
            fours.append(at(2 * block + part, dp))

    def remote(src, dst, send, recv, device_id):
        return pltpu.make_async_remote_copy(
            src_ref=src, dst_ref=dst, send_sem=send, recv_sem=recv, device_id=device_id, device_id_type=MESH
        )

    load_k = pltpu.make_async_copy(k_hbm, kv.at[0, 0:ROWS], in_sem.at[0])
    load_v = pltpu.make_async_copy(v_hbm, kv.at[1, 0:ROWS], in_sem.at[1])
    load_d = pltpu.make_async_copy(d_hbm, d, in_sem.at[2])
    load_w = pltpu.make_async_copy(w_hbm, w, in_sem.at[3])
    load_q = pltpu.make_async_copy(q_hbm, q, in_sem.at[4])
    for load in (load_k, load_v, load_d, load_w, load_q):
        load.start()
    barrier = pltpu.get_barrier_semaphore()
    partners = [right, left, twin, at_ya, at_yb] + fours
    for partner in partners:
        pl.semaphore_signal(barrier, inc=1, device_id=partner, device_id_type=MESH)

    def greet(number, carry):
        pl.semaphore_signal(barrier, inc=1, device_id=at(lax.rem(seq + number, N_SEQ), dp), device_id_type=MESH)
        return carry

    lax.fori_loop(1, N_SEQ, greet, 0)

    matrix, scale = pool_matrix()
    pooled = []
    for part, load in ((0, load_k), (1, load_v)):
        load.wait()
        sums = dot_nn(matrix, kv[part, 0:ROWS, :]) * scale
        kv[part, OWN1:LEFT, :] = sums[0:96].astype(BF16)
        rim[0, 16 * part : 16 * part + 16] = kv[part, 0:16, :]
        rim[1, 16 * part : 16 * part + 16] = kv[part, 112:128, :]
        pooled.append(sums)

    def of_both(row):
        return jnp.concatenate([sums[row : row + 8] for sums in pooled], axis=0).astype(BF16)

    for side, rows in ((0, (8, 72, 104)), (1, (48, 80, 96))):
        for number, row in enumerate(rows):
            rim[side, 32 + 16 * number : 48 + 16 * number] = of_both(row)
    four[...] = of_both(112)

    pl.semaphore_wait(barrier, len(partners) + N_SEQ - 1)

    def part_of(z_at, step):
        return lax.rem(lax.div(z_at, 2) + 2 - step + 3 * lax.div(step, 2) - 2 * lax.div(step, 3), STEPS)

    def lanes_at(z_at, step):
        return pl.ds(pl.multiple_of(part_of(z_at, step) * WIDE, WIDE), WIDE)

    def lanes_of(step):
        return lanes_at(z, step)

    def pair_lanes(step, pair):
        return pl.ds(pl.multiple_of(part_of(z, step) * WIDE + pair * PAIR, PAIR), PAIR)

    def rim_copies(step, lanes_to):
        copies = []
        for side, partner in ((0, left), (1, right)):
            lanes = lanes_to(partner, step)
            copies.append(
                remote(
                    rim.at[side, :, lanes],
                    rim_in.at[1 - side, :, lanes],
                    rim_s.at[side],
                    rim_r.at[side * STEPS + step],
                    partner,
                )
            )
        return copies

    def four_copies(step, lanes_to):
        copies = []
        for number, partner in enumerate(fours):
            slot = parity + (2 if number < 2 else 0)
            lanes = lanes_to(partner, step)
            copies.append(
                remote(
                    four.at[:, lanes],
                    four_in.at[slot, :, lanes],
                    four_s.at[number],
                    four_r.at[slot * STEPS + step],
                    partner,
                )
            )
        return copies

    for step in range(STEPS):
        for copies in (four_copies, rim_copies):
            for copy in copies(step, lambda partner, step: lanes_at(lax.div(partner["seq"], X), step)):
                copy.start()

    def wait_rims(step):
        lanes = lanes_of(step)
        for copy in rim_copies(step, lambda partner, step: lanes):
            copy.wait_recv()
        for side, row in ((0, LEFT), (1, RIGHT)):
            rows = dot_nn(unfold[side], rim_in[side, :, lanes]) * rim_scale(side)
            kv[0, row : row + 64, lanes] = rows[0:64].astype(BF16)
            kv[1, row : row + 64, lanes] = rows[64:128].astype(BF16)
        for number in range(4):
            remote(
                four.at[:, lanes],
                four_in.at[number, :, lanes],
                four_s.at[number],
                four_r.at[number * STEPS + step],
                fours[number],
            ).wait_recv()
        for side, row in ((0, LEFT4), (1, RIGHT4)):
            one = four_in[2 * side, :, lanes].astype(F32)
            two = four_in[2 * side + 1, :, lanes].astype(F32)
            for part in (0, 1):
                kv[part, row : row + 16, lanes] = jnp.concatenate(
                    [one[8 * part : 8 * part + 8], two[8 * part : 8 * part + 8]], axis=0
                ).astype(BF16)

    load_d.wait()
    mine_rows = pl.ds(pl.multiple_of(core * ROWS, ROWS), ROWS)
    twin_columns = []
    for number, y_to in enumerate((y, ya, yb, yo)):
        columns = slice(number * PAIR, (number + 1) * PAIR)
        theirs = pl.ds(pl.multiple_of(y_to * 256 + (1 - core) * PAIR, PAIR), PAIR)
        copy = remote(
            d.at[:, theirs], pairs_d.at[mine_rows, columns], d2_s.at[number], d2_r.at[number], twin
        )
        copy.start()
        twin_columns.append(copy)

    fill_bias(bias, seq)
    spread[...] = spread_matrix()
    for side in (0, 1):
        unfold[side] = rim_matrix((ROWS, SENT), 0, side)
        fold[side] = rim_matrix((SENT, ROWS), 1, side)
    for part in (0, 1):
        spread_back[part] = jnp.concatenate(spread_sent(part), axis=1).astype(BF16)
    for number, y_to in enumerate((y, ya, yb, yo)):
        ours = pl.ds(pl.multiple_of(y_to * 256 + core * PAIR, PAIR), PAIR)
        pairs_d[mine_rows, number * PAIR : (number + 1) * PAIR] = d[:, ours]
    load_w.wait()
    for column in range(0, WIDTH, 256):
        g[:, column : column + 256] = dot_nt(d[...], w[column : column + 256, :]).astype(BF16)
    load_q.wait()

    for copy in twin_columns:
        copy.wait_recv()

    mine_lanes = pl.ds(pl.multiple_of(core * ROWS, ROWS), ROWS)

    def copy_a(step):
        block = pairs_a.at[step, :, mine_lanes]
        return remote(block, block, a_s.at[step], a_r.at[step], twin)

    def copies_y1(step):
        return (
            remote(y1_out.at[step, 0], y1_in.at[step, 0], y1_s.at[2 * step], y1_r.at[2 * step], at_ya),
            remote(y1_out.at[step, 1], y1_in.at[step, 1], y1_s.at[2 * step + 1], y1_r.at[2 * step + 1], at_yb),
        )

    def copies_y2(step):
        return (
            remote(y2_out.at[step, 0], y2_in.at[step, 0], y2_s.at[2 * step], y2_r.at[2 * step], at_yb),
            remote(y2_out.at[step, 1], y2_in.at[step, 1], y2_s.at[2 * step + 1], y2_r.at[2 * step + 1], at_ya),
        )

    odd_z = lax.rem(z, 2)

    def send_z(step, pair):
        z_to = 2 * part_of(z, step) + pair
        last = lax.div(step, STEPS - 1)
        same = last * (odd_z if pair else 1 - odd_z)

        def copy(apart):
            x_to = lax.rem(x + apart, X)
            rows = pl.ds(pl.multiple_of(pair * PAIR + x_to * 32, 32), 32)
            slot = 8 * step + (1 - last) * 4 * odd_z + 3 * same + apart
            return remote(
                z_out.at[step, rows], z_in.at[slot], z_s.at[0], z_r.at[0], at(z_to * X + x_to, dp)
            )

        @pl.when(same == 0)
        def _():
            copy(0).start()

        for apart in range(1, X):
            copy(apart).start()

    def forward(step):
        lanes = [pair_lanes(step, pair) for pair in (0, 1)]
        query_rows = [two_heads(q[:, at_lanes], 0.125) for at_lanes in lanes]
        scores = [dot_nt(kv[0, :, at_lanes], rows) + bias[...] for at_lanes, rows in zip(lanes, query_rows)]
        tops = [jnp.max(score, axis=0, keepdims=True) for score in scores]
        exponents = [jnp.exp(score - top) for score, top in zip(scores, tops)]
        shares = [1.0 / jnp.sum(exponent, axis=0, keepdims=True) for exponent in exponents]
        normal = [exponent * share for exponent, share in zip(exponents, shares)]
        halves = [weight.astype(BF16) for weight in normal]
        attended = [
            one_of_two(dot_tn(kv[1, :, at_lanes], half)).astype(BF16) for at_lanes, half in zip(lanes, halves)
        ]
        for pair in (0, 1):
            weights[2 * step + pair] = normal[pair]
            weights_half[2 * step + pair] = halves[pair]
            pairs_a[step, pair * PAIR : (pair + 1) * PAIR, mine_lanes] = attended[pair]
        copy_a(step).start()

    def project(step):
        copy_a(step).wait_recv()
        partial = dot_nn(pairs_a[step], pairs_d[...])
        kept[step] = partial[:, 0:128]
        kept2[step, 0:128] = partial[0:128, 256:384]
        kept2[step, 128:256] = partial[128:256, 128:256]
        y1_out[step, 0, 0:128] = partial[0:128, 128:256].astype(BF16)
        y1_out[step, 0, 128:256] = partial[0:128, 384:512].astype(BF16)
        y1_out[step, 1, 0:128] = partial[128:256, 256:384].astype(BF16)
        y1_out[step, 1, 128:256] = partial[128:256, 384:512].astype(BF16)
        for copy in copies_y1(step):
            copy.start()

    def fold_y1(step):
        for copy in copies_y1(step):
            copy.wait_recv()
        for half in (0, 1):
            rows = slice(128 * half, 128 * half + 128)
            kept[step, rows] = kept[step, rows] + y1_in[step, half, 0:128].astype(F32)
            y2_out[step, half] = (kept2[step, rows] + y1_in[step, half, 128:256].astype(F32)).astype(BF16)
        for copy in copies_y2(step):
            copy.start()

    def fold_y2(step):
        for copy in copies_y2(step):
            copy.wait_recv()
        for half in (0, 1):
            rows = slice(128 * half, 128 * half + 128)
            total = kept[step, rows] + y2_in[step, half].astype(F32)
            kept[step, rows] = total
            z_out[step, rows] = total.astype(BF16)
        for pair in (0, 1):
            send_z(step, pair)

    def backward_rims(step):
        steps = (2 * step, 2 * step + 1)
        lanes = [pair_lanes(step, pair) for pair in (0, 1)]
        query_rows = [two_heads(q[:, at_lanes], 0.125) for at_lanes in lanes]
        grad_rows = [two_heads(g[:, at_lanes], 1.0) for at_lanes in lanes]
        d_probs = [dot_nt(kv[1, :, at_lanes], rows) for at_lanes, rows in zip(lanes, grad_rows)]
        normal = [weights[number] for number in steps]
        own_scale = level_scale(lax.rem(lax.broadcasted_iota(jnp.int32, (ROWS, 1), 0), 64) // 16)
        deltas = [jnp.sum(weight * d_prob, axis=0, keepdims=True) for weight, d_prob in zip(normal, d_probs)]
        d_scores = [
            (weight * (d_prob - delta)).astype(BF16) for weight, d_prob, delta in zip(normal, d_probs, deltas)
        ]
        d_keys = [dot_nn(d_score[LEFT:], rows) for d_score, rows in zip(d_scores, query_rows)]
        d_values = [dot_nn(weights_half[number, LEFT:, :], rows) for number, rows in zip(steps, grad_rows)]
        for number, at_lanes, d_score, d_key, d_value in zip(steps, lanes, d_scores, d_keys, d_values):
            grad_scores[number] = d_score
            for side in (0, 1):
                rows = slice(64 * side, 64 * side + 64)
                grads = jnp.concatenate([d_key[rows], d_value[rows]], axis=0) * own_scale
                back_rim[side, :, at_lanes] = dot_nn(fold[side], grads.astype(BF16)).astype(BF16)
            for number in range(4):
                rows = slice(128 + 8 * number, 136 + 8 * number)
                both = jnp.concatenate([d_key[rows], d_value[rows]], axis=0) * 0.25
                back_four[number, :, at_lanes] = both.astype(BF16)
        for at_lanes in [lanes_of(step)]:
            remote(
                back_rim.at[0, :, at_lanes], back_in.at[0:SENT, at_lanes], back_s.at[0], back_r.at[0], left
            ).start()
            remote(
                back_rim.at[1, :, at_lanes], back_in.at[SENT : 2 * SENT, at_lanes], back_s.at[1], back_r.at[1], right
            ).start()
            for number, partner in enumerate(fours):
                slot = parity + (2 if number < 2 else 0)
                remote(
                    back_four.at[number, :, at_lanes],
                    back_four_in.at[slot, :, at_lanes],
                    bfour_s.at[number],
                    bfour_r.at[slot],
                    partner,
                ).start()

    def backward_own(step):
        steps = (2 * step, 2 * step + 1)
        lanes = [pair_lanes(step, pair) for pair in (0, 1)]
        query_rows = [two_heads(q[:, at_lanes], 0.125) for at_lanes in lanes]
        grad_rows = [two_heads(g[:, at_lanes], 1.0) for at_lanes in lanes]
        d_queries = [
            one_of_two(dot_tn(kv[0, :, at_lanes], grad_scores[number])) * 0.125 for number, at_lanes in zip(steps, lanes)
        ]
        d_keys = [dot_nn(grad_scores[number, 0:LEFT, :], rows) for number, rows in zip(steps, query_rows)]
        d_values = [dot_nn(weights_half[number, 0:LEFT, :], rows) for number, rows in zip(steps, grad_rows)]
        for at_lanes, d_query, d_key, d_value in zip(lanes, d_queries, d_keys, d_values):
            dq_ref[:, at_lanes] = d_query.T.astype(BF16)
            for part, grad in ((0, d_key), (1, d_value)):
                own[part, :, at_lanes] = grad[0:ROWS]
                back[part, 0:64, at_lanes] = (grad[OWN1:OWN2] * 2.0 ** (-0.5)).astype(BF16)
                back[part, 64:96, at_lanes] = (grad[OWN2:LEFT] * 0.5).astype(BF16)

    def forward_step(step, carry):
        wait_rims(step)
        forward(step)

        @pl.when(step >= 1)
        def _():
            project(step - 1)

        return carry

    def rims_step(step, carry):
        backward_rims(step)

        @pl.when(step == 0)
        def _():
            project(step + 3)

        @pl.when(lax.rem(step, 2) == 1)
        def _():
            fold_y1(step // 2)

        return carry

    def own_step(step, carry):
        backward_own(step)

        @pl.when(lax.rem(step, 2) == 1)
        def _():
            fold_y2(step // 2)
            fold_y1(2 + step // 2)

        return carry

    lax.fori_loop(0, STEPS, forward_step, 0)
    lax.fori_loop(0, STEPS, rims_step, 0)
    lax.fori_loop(0, STEPS, own_step, 0)
    for step in (2, 3):
        fold_y2(step)

    rim_left = remote(back_rim.at[0], back_in.at[0:SENT], back_s.at[0], back_r.at[0], left)
    rim_right = remote(back_rim.at[1], back_in.at[SENT : 2 * SENT], back_s.at[1], back_r.at[1], right)
    rim_left.wait_recv()
    rim_right.wait_recv()
    for number in range(4):
        remote(
            back_four.at[number], back_four_in.at[number], bfour_s.at[number], bfour_r.at[number], fours[number]
        ).wait_recv()
    for part, out in ((0, dk_ref), (1, dv_ref)):
        for column in range(0, WIDTH, 256):
            columns = slice(column, column + 256)
            rows4 = [back_four_in[number, :, columns].astype(F32)[8 * part : 8 * part + 8] for number in range(4)]
            back[part, 96:128, columns] = jnp.concatenate(rows4, axis=0).astype(BF16)
            total = own[part, :, columns] + dot_nn(spread[...], back[part, :, columns])
            out[:, columns] = (total + dot_nn(spread_back[part], back_in[:, columns])).astype(BF16)

    all_z = remote(z_in, z_in, z_s.at[0], z_r.at[0], right)
    all_z.wait_recv()
    mine = kept[STEPS - 1, pl.ds(pl.multiple_of(odd_z * PAIR + x * 32, 32), 32), :]
    gw_ref[...] = (mine + jnp.sum(z_in[...].astype(F32), axis=0)) * FACTOR

    sent_rims = [
        remote(rim.at[side], rim_in.at[side], rim_s.at[side], rim_r.at[0], right) for side in (0, 1)
    ]
    sent_four = [
        remote(four, four_in.at[number], four_s.at[number], four_r.at[number], fours[number]) for number in range(4)
    ]
    for copy in sent_rims + sent_four + twin_columns + [rim_left, rim_right, all_z]:
        copy.wait_send()
    for number in range(4):
        remote(
            back_four.at[number], back_four_in.at[number], bfour_s.at[number], bfour_r.at[number], fours[number]
        ).wait_send()

    def wait_sends(step, carry):
        copy_a(step).wait_send()
        for copy in copies_y1(step) + copies_y2(step):
            copy.wait_send()
        return carry

    lax.fori_loop(0, STEPS, wait_sends, 0)


def hand_on(*refs):
    given, results, sems = refs[0:4], refs[4:8], refs[8]
    stores = [pltpu.make_async_copy(given[i], results[i], sems.at[i]) for i in range(4)]
    for store in stores:
        store.start()
    for store in stores:
        store.wait()


def on_device(queries, keys, values, d_out, w_out):
    dma = pltpu.SemaphoreType.DMA
    any_space = pl.BlockSpec(memory_space=pl.ANY)
    rows_shape = jax.ShapeDtypeStruct((ROWS, WIDTH), BF16)
    grad_shape = jax.ShapeDtypeStruct((32, 128), F32)
    results = (rows_shape, rows_shape, rows_shape, grad_shape)
    held = tuple(pltpu.VMEM(result.shape, result.dtype) for result in results)
    vmem = pl.BlockSpec(memory_space=pltpu.VMEM)
    outs = pl.pallas_call(
        kernel,
        out_shape=held,
        in_specs=[any_space] * 5,
        out_specs=(vmem,) * 4,
        scratch_shapes=[
            pltpu.VMEM((ROWS, WIDTH), BF16),
            pltpu.VMEM((ROWS, WIDTH), BF16),
            pltpu.VMEM((WIDTH, WIDTH), BF16),
            pltpu.VMEM((ROWS, WIDTH), BF16),
            pltpu.VMEM((2, KEYS, WIDTH), BF16),
            pltpu.VMEM((KEYS, 2 * ROWS), F32),
            pltpu.VMEM((ROWS, ROWS), BF16),
            pltpu.VMEM((2, ROWS, 2 * SENT), BF16),
            pltpu.VMEM((2, ROWS, SENT), BF16),
            pltpu.VMEM((2, SENT, ROWS), BF16),
            pltpu.VMEM((2, SENT, WIDTH), BF16),
            pltpu.VMEM((2, SENT, WIDTH), BF16),
            pltpu.VMEM((16, WIDTH), BF16),
            pltpu.VMEM((4, 16, WIDTH), BF16),
            pltpu.VMEM((PAIRS, KEYS, 2 * ROWS), F32),
            pltpu.VMEM((PAIRS, KEYS, 2 * ROWS), BF16),
            pltpu.VMEM((PAIRS, KEYS, 2 * ROWS), BF16),
            pltpu.VMEM((2, ROWS, WIDTH), F32),
            pltpu.VMEM((2, ROWS, WIDTH), BF16),
            pltpu.VMEM((2 * SENT, WIDTH), BF16),
            pltpu.VMEM((2, SENT, WIDTH), BF16),
            pltpu.VMEM((4, 16, WIDTH), BF16),
            pltpu.VMEM((4, 16, WIDTH), BF16),
            pltpu.VMEM((STEPS, WIDE, 2 * ROWS), BF16),
            pltpu.VMEM((2 * ROWS, 512), BF16),
            pltpu.VMEM((STEPS, WIDE, 128), F32),
            pltpu.VMEM((STEPS, WIDE, 128), F32),
            pltpu.VMEM((STEPS, 2, WIDE, 128), BF16),
            pltpu.VMEM((STEPS, 2, WIDE, 128), BF16),
            pltpu.VMEM((STEPS, 2, 128, 128), BF16),
            pltpu.VMEM((STEPS, 2, 128, 128), BF16),
            pltpu.VMEM((STEPS, WIDE, 128), BF16),
            pltpu.VMEM((N_SEQ - 1, 32, 128), BF16),
            dma((5,)),
            dma((2,)), dma((2 * STEPS,)),
            dma((4,)), dma((4 * STEPS,)),
            dma((4,)), dma((4,)),
            dma((STEPS,)), dma((STEPS,)),
            dma((2 * STEPS,)), dma((2 * STEPS,)),
            dma((2 * STEPS,)), dma((2 * STEPS,)),
            dma((1,)), dma((1,)),
            dma((2,)), dma((2,)),
            dma((4,)), dma((4,)),
        ],
        compiler_params=pltpu.CompilerParams(
            collective_id=0, has_side_effects=True, vmem_limit_bytes=VMEM_BYTES
        ),
    )(queries[0], keys[0], values[0], d_out[0], w_out)
    d_queries, d_keys, d_values, grad_w = pl.pallas_call(
        hand_on,
        out_shape=results,
        in_specs=[any_space] * 4,
        out_specs=(any_space,) * 4,
        scratch_shapes=[dma((4,))],
        compiler_params=pltpu.CompilerParams(vmem_limit_bytes=4 * 1024 * 1024),
    )(*outs)
    return d_queries[None], d_keys[None], d_values[None], grad_w


def solution(mesh):
    placed = P("dp", "seq", None)
    return jax.shard_map(
        on_device,
        mesh=mesh,
        in_specs=(placed, placed, placed, placed, P()),
        out_specs=(placed, placed, placed, P("seq", "dp")),
        check_vma=False,
    )
```

profile of v0, /device:TPU:2, one launch (start us, length us, event | category | flops | bytes accessed | tf_op | source)
XLA Modules:
  0.0 41.4 jit_solution(4609482096007959107)
XLA Ops:
  0.6 39.8 %shard_map.84 = (bf16[128,1024]{1,0:T(8,128)(2,1)S(1)}, bf16[128,1024]{1,0:T(8,128)(2,1)S(1)}, bf16[128,1024]{1,0:T(8,128)(2,1)S(1)}, f32[32,128]{1,0:T(8,128)S(1)}) custom-call(bf16[128,1024]{1,0:T(8,128)(2,1)} %bitcast.7, bf16[128,1024]{1,0:T(8,128)(2,1)} %bitcast.8, bf16[128,1024]{1,0:T(8,128)(2,1)} %bitcast.9, bf16[128,1024]{1,0:T(8,128)(2,1)} %bitcast.10, ...), custom_call_target="tpu_custom_call" | custom-call | tf_op jit(solution)/shard_map/pallas_call | solution.py:577
  40.4 0.9 %shard_map.85 = (bf16[128,1024]{1,0:T(8,128)(2,1)}, bf16[128,1024]{1,0:T(8,128)(2,1)}, bf16[128,1024]{1,0:T(8,128)(2,1)}, f32[32,128]{1,0:T(8,128)}) custom-call(bf16[128,1024]{1,0:T(8,128)(2,1)S(1)} %get-tuple-element.12.refs_0_, bf16[128,1024]{1,0:T(8,128)(2,1)S(1)} %get-tuple-element.13.refs_1_, bf16[128,1024]{1,0:T(8,128)(2,1)S(1)} %get-tuple-element.14.refs_2_, ...), custom_call_target="tpu_custom_call" | custom-call | tf_op jit(solution)/shard_map/pallas_call | solution.py:631
where the time goes:
time: 41.4 us
  Pallas kernels  40.7 us (98%)
  between operations  0.64 us (2%)
    pallas_call x1, Pallas kernels, on_device(): pl.pallas_call(kernel, out_shape=held, in_specs=[any_space] * 5, out_spec...  39.8 us
    pallas_call x1, Pallas kernels, on_device(): pl.pallas_call(hand_on, out_shape=results, in_specs=[any_space] * 4, out_...  0.91 us

commit v1 on v0

--- a/solution.py
+++ b/solution.py
@@ -149,7 +149,7 @@
 
 def kernel(
     q_hbm, k_hbm, v_hbm, d_hbm, w_hbm,
-    dq_ref, dk_ref, dv_ref, gw_ref, q, d, w, g, kv, bias, spread, spread_back, unfold, fold,
+    dq_ref, dk_ref, dv_ref, gw_ref, q, d, w, g, kv, bias, spread, spread_back, unfold, fold, scale_in, scale_out,
     rim, rim_in, four, four_in,
     weights, weights_half, grad_scores, own, back, back_in, back_rim, back_four, back_four_in,
     pairs_a, pairs_d, kept, kept2, y1_out, y1_in, y2_out, y2_in, z_out, z_in,
@@ -276,7 +276,7 @@
         for copy in rim_copies(step, lambda partner, step: lanes):
             copy.wait_recv()
         for side, row in ((0, LEFT), (1, RIGHT)):
-            rows = dot_nn(unfold[side], rim_in[side, :, lanes]) * rim_scale(side)
+            rows = dot_nn(unfold[side], rim_in[side, :, lanes]) * scale_in[side]
             kv[0, row : row + 64, lanes] = rows[0:64].astype(BF16)
             kv[1, row : row + 64, lanes] = rows[64:128].astype(BF16)
         for number in range(4):
@@ -308,12 +308,11 @@
         twin_columns.append(copy)
 
     fill_bias(bias, seq)
-    spread[...] = spread_matrix()
+    scale_out[...] = level_scale(lax.rem(lax.broadcasted_iota(jnp.int32, (ROWS, PAIR), 0), 64) // 16)
     for side in (0, 1):
+        scale_in[side] = jnp.broadcast_to(rim_scale(side), (ROWS, WIDE))
         unfold[side] = rim_matrix((ROWS, SENT), 0, side)
         fold[side] = rim_matrix((SENT, ROWS), 1, side)
-    for part in (0, 1):
-        spread_back[part] = jnp.concatenate(spread_sent(part), axis=1).astype(BF16)
     for number, y_to in enumerate((y, ya, yb, yo)):
         ours = pl.ds(pl.multiple_of(y_to * 256 + core * PAIR, PAIR), PAIR)
         pairs_d[mine_rows, number * PAIR : (number + 1) * PAIR] = d[:, ours]
@@ -424,7 +423,6 @@
         grad_rows = [two_heads(g[:, at_lanes], 1.0) for at_lanes in lanes]
         d_probs = [dot_nt(kv[1, :, at_lanes], rows) for at_lanes, rows in zip(lanes, grad_rows)]
         normal = [weights[number] for number in steps]
-        own_scale = level_scale(lax.rem(lax.broadcasted_iota(jnp.int32, (ROWS, 1), 0), 64) // 16)
         deltas = [jnp.sum(weight * d_prob, axis=0, keepdims=True) for weight, d_prob in zip(normal, d_probs)]
         d_scores = [
             (weight * (d_prob - delta)).astype(BF16) for weight, d_prob, delta in zip(normal, d_probs, deltas)
@@ -435,7 +433,7 @@
             grad_scores[number] = d_score
             for side in (0, 1):
                 rows = slice(64 * side, 64 * side + 64)
-                grads = jnp.concatenate([d_key[rows], d_value[rows]], axis=0) * own_scale
+                grads = jnp.concatenate([d_key[rows], d_value[rows]], axis=0) * scale_out[...]
                 back_rim[side, :, at_lanes] = dot_nn(fold[side], grads.astype(BF16)).astype(BF16)
             for number in range(4):
                 rows = slice(128 + 8 * number, 136 + 8 * number)
@@ -514,6 +512,9 @@
     for step in (2, 3):
         fold_y2(step)
 
+    spread[...] = spread_matrix()
+    for part in (0, 1):
+        spread_back[part] = jnp.concatenate(spread_sent(part), axis=1).astype(BF16)
     rim_left = remote(back_rim.at[0], back_in.at[0:SENT], back_s.at[0], back_r.at[0], left)
     rim_right = remote(back_rim.at[1], back_in.at[SENT : 2 * SENT], back_s.at[1], back_r.at[1], right)
     rim_left.wait_recv()
@@ -590,6 +591,8 @@
             pltpu.VMEM((2, ROWS, 2 * SENT), BF16),
             pltpu.VMEM((2, ROWS, SENT), BF16),
             pltpu.VMEM((2, SENT, ROWS), BF16),
+            pltpu.VMEM((2, ROWS, WIDE), F32),
+            pltpu.VMEM((ROWS, PAIR), F32),
             pltpu.VMEM((2, SENT, WIDTH), BF16),
             pltpu.VMEM((2, SENT, WIDTH), BF16),
             pltpu.VMEM((16, WIDTH), BF16),

time: 41.4 us -> 41.4 us (level)
  no operation moved by 1% of the time
where the time goes in v1:
time: 41.4 us; the launch traced here: 41.3 us
  Pallas kernels  40.7 us (98%)
  between operations  0.64 us (2%)
    pallas_call x1, Pallas kernels, on_device(): pl.pallas_call(kernel, out_shape=held, in_specs=[any_space] * 5, out_spec...  39.8 us
    pallas_call x1, Pallas kernels, on_device(): pl.pallas_call(hand_on, out_shape=results, in_specs=[any_space] * 4, out_...  0.91 us

profile of v1, /device:TPU:2, one launch (start us, length us, event | category | flops | bytes accessed | tf_op | source)
XLA Modules:
  0.0 41.3 jit_solution(8748137014389665202)
XLA Ops:
  0.6 39.8 %shard_map.84 = (bf16[128,1024]{1,0:T(8,128)(2,1)S(1)}, bf16[128,1024]{1,0:T(8,128)(2,1)S(1)}, bf16[128,1024]{1,0:T(8,128)(2,1)S(1)}, f32[32,128]{1,0:T(8,128)S(1)}) custom-call(bf16[128,1024]{1,0:T(8,128)(2,1)} %bitcast.7, bf16[128,1024]{1,0:T(8,128)(2,1)} %bitcast.8, bf16[128,1024]{1,0:T(8,128)(2,1)} %bitcast.9, bf16[128,1024]{1,0:T(8,128)(2,1)} %bitcast.10, ...), custom_call_target="tpu_custom_call" | custom-call | tf_op jit(solution)/shard_map/pallas_call | solution.py:578
  40.4 0.9 %shard_map.85 = (bf16[128,1024]{1,0:T(8,128)(2,1)}, bf16[128,1024]{1,0:T(8,128)(2,1)}, bf16[128,1024]{1,0:T(8,128)(2,1)}, f32[32,128]{1,0:T(8,128)}) custom-call(bf16[128,1024]{1,0:T(8,128)(2,1)S(1)} %get-tuple-element.12.refs_0_, bf16[128,1024]{1,0:T(8,128)(2,1)S(1)} %get-tuple-element.13.refs_1_, bf16[128,1024]{1,0:T(8,128)(2,1)S(1)} %get-tuple-element.14.refs_2_, ...), custom_call_target="tpu_custom_call" | custom-call | tf_op jit(solution)/shard_map/pallas_call | solution.py:634
